TPU v7x, 512 devices: a whole 4x8x8 slice. The times are simulated.
512 devices in a mesh: row: 16 (over y, core), col: 32 (over z, x).
Axes of the slice: x: 4, y: 8, z: 8, core: 2. Of those that a mesh axis runs over, the one named last changes fastest.
Arguments:
- grad: bfloat16 [6144, 6144], P('col', 'row'), may hold values from -6 to 6
- basis: bfloat16 [6144, 6144], P('col', 'row'), may hold values from -0.078125 to 0.078125
- moment: float32 [6144, 6144], P('col', 'row'), may hold values from -6 to 6
- second: float32 [6144, 6144], P('col', 'row'), may hold values from 0.1 to 10
Outputs:
- update: bfloat16 [6144, 6144], P('col', 'row')
- moment_new: float32 [6144, 6144], P('col', 'row')
- second_new: float32 [6144, 6144], P('col', 'row')
All inputs are finite; a program needn't handle non-finite values.
Results may differ from a plain program's by a relative error of at most 0.018.
Values may be sent and summed in bfloat16 or wider, within the bound.
A program may use at most 64 MiB of HBM per device.

v0:
```python
import jax
import jax.numpy as jnp
from jax import lax
from jax.sharding import PartitionSpec as P


def per_device(grad, basis, moment, second):
    grad_panel = lax.all_gather(grad, "row", axis=1, tiled=True)
    basis_panel = lax.all_gather(basis, "col", axis=0, tiled=True)
    rotated = jnp.dot(grad_panel, basis_panel, preferred_element_type=jnp.float32)
    moment_new = 0.9 * moment + 0.1 * rotated
    second_new = 0.95 * second + 0.05 * rotated * rotated
    corr_one = 1.0 - 0.9**10
    corr_two = 1.0 - 0.95**10
    direction = (moment_new / corr_one / (jnp.sqrt(second_new / corr_two) + 1e-08)).astype(
        jnp.bfloat16
    )
    partial_value = lax.dot_general(
        direction, basis_panel, (((1,), (1,)), ((), ())), preferred_element_type=jnp.float32
    )
    update = lax.psum_scatter(
        partial_value.astype(jnp.bfloat16), "row", scatter_dimension=1, tiled=True
    )
    return (update, moment_new, second_new)


def solution(mesh):
    return jax.shard_map(
        per_device,
        mesh=mesh,
        in_specs=(P("col", "row"), P("col", "row"), P("col", "row"), P("col", "row")),
        out_specs=(P("col", "row"), P("col", "row"), P("col", "row")),
        check_vma=False,
    )
```

profile of v0, /device:TPU:6, one launch (start us, length us, event | category | flops | bytes accessed | tf_op | source)
XLA Modules:
  0.0 226.7 jit_solution(7356775681142423844)
XLA Ops:
  7.2 0.0 all-gather.3.cloned.1.call-start
  7.2 0.7 all-gather.3.cloned.1.call-update
  7.9 0.0 all-gather.5.cloned.1.call-start
  7.9 0.7 all-gather.5.cloned.1.call-update
  8.6 0.0 reduce-scatter.4.cloned.1.call-start
  8.7 48.2 %all-gather.3.cloned.1.call-done = bf16[192,6144]{1,0:T(8,128)(2,1)} async-done(((bf16[192,384]{1,0:T(8,128)(2,1)}), bf16[192,6144]{1,0:T(8,128)(2,1)}) %all-gather.3.cloned.1.call-update) | async-done | bytes 2359312 | tf_op jit(solution)/shard_map/all_gather | solution.py:8
  56.9 90.5 %all-gather.5.cloned.1.call-done = bf16[6144,384]{1,0:T(8,128)(2,1)} async-done(((bf16[192,384]{1,0:T(8,128)(2,1)}), bf16[6144,384]{1,0:T(8,128)(2,1)}) %all-gather.5.cloned.1.call-update) | async-done | bytes 4718608 | tf_op jit(solution)/shard_map/all_gather | solution.py:9
  147.5 0.0 copy-start
  147.5 4.7 %multiply_add_fusion = (f32[192,384]{1,0:T(8,128)S(1)}, f32[192,384]{1,0:T(8,128)S(1)}) fusion(f32[192,384]{1,0:T(8,128)} %param.6, f32[192,384]{1,0:T(8,128)} %param.7, bf16[192,6144]{1,0:T(8,128)(2,1)} %all-gather.3.cloned.1.call-done, bf16[6144,384]{1,0:T(8,128)(2,1)} %all-gather.5.cloned.1.call-done), kind=kOutput, calls=%fused_computation.4 | convolution fusion | flops 906485760 | bytes 8257536 | tf_op jit(solution)/shard_map/dot_general | solution.py:10
  152.2 0.0 copy-start.1
  152.2 0.0 copy-start.2
  152.2 0.0 copy-done
  152.2 1.9 convolution_convert_fusion
  154.1 2.8 %copy.7 = bf16[192,6144]{0,1:T(8,128)(2,1)} copy(bf16[192,6144]{1,0:T(8,128)(2,1)S(1)} %convolution_convert_fusion) | data formatting | bytes 4718592
  156.9 0.0 copy-done.1
  156.9 0.0 copy-done.2
  156.9 0.0 reduce-scatter.4.cloned.1.call-update
  156.9 61.6 %reduce-scatter.4.cloned.1.call-done = bf16[384,192]{1,0:T(8,128)(2,1)} async-done(((bf16[6144,192]{1,0:T(8,128)(2,1)}), bf16[384,192]{1,0:T(8,128)(2,1)}) %reduce-scatter.4.cloned.1.call-update) | async-done | bytes 147472
  218.5 1.7 copy.8
Async XLA Ops:
  7.2 49.8 %all-gather.3.cloned.1.call-start = ((), (), s32[]{:S(2)}) async-start(), calls=%async_computation.1 | async-start | bytes 2506752 | tf_op jit(solution)/shard_map/all_gather | solution.py:8
  7.9 139.6 %all-gather.5.cloned.1.call-start = ((), (), s32[]{:S(2)}) async-start(), calls=%async_computation.2 | async-start | bytes 4866048 | tf_op jit(solution)/shard_map/all_gather | solution.py:9
  8.6 209.8 %reduce-scatter.4.cloned.1.call-start = ((), (), s32[]{:S(2)}) async-start(), calls=%async_computation.3 | async-start | bytes 3342336
  147.5 4.7 %copy-start = (bf16[6144,384]{1,0:T(8,128)(2,1)S(1)}, bf16[6144,384]{1,0:T(8,128)(2,1)}, u32[]{:S(2)}) copy-start(bf16[6144,384]{1,0:T(8,128)(2,1)} %all-gather.5.cloned.1.call-done) | copy-start | bytes 14155780
  152.2 4.7 %copy-start.1 = (f32[192,384]{1,0:T(8,128)}, f32[192,384]{1,0:T(8,128)S(1)}, u32[]{:S(2)}) copy-start(f32[192,384]{1,0:T(8,128)S(1)} %get-tuple-element.3) | copy-start | bytes 884740
  152.2 4.7 %copy-start.2 = (f32[192,384]{1,0:T(8,128)}, f32[192,384]{1,0:T(8,128)S(1)}, u32[]{:S(2)}) copy-start(f32[192,384]{1,0:T(8,128)S(1)} %get-tuple-element.4) | copy-start | bytes 884740
Sparse Core Ops, SparseCore 0:
  10.1 46.8 all-gather.2
  60.1 87.3 all-gather.4
  157.0 61.4 reduce-scatter.3
where the time goes:
time: 227 us
  waiting for transfers between devices  202 us (89%)
  between operations  13.8 us (6%)
  matrix products  6.57 us (3%)
  local copies, waits for them, and re-layouts  4.51 us (2%)
    all_gather x1, waiting for transfers between devices, per_device(): basis_panel = lax.all_gather(basis, 'col', axis=0, tiled=True)  90.5 us
    unnamed x4, waiting for transfers between devices  63 us
    all_gather x1, waiting for transfers between devices, per_device(): grad_panel = lax.all_gather(grad, 'row', axis=1, tiled=True)  48.2 us
    dot_general x1, matrix products, per_device(): jnp.dot(grad_panel, basis_panel, preferred_element_type=jnp.float32)  4.7 us
  transfers between devices with their start and end apart: 3, of which 3 were waited for; matrix products, arithmetic and copies ran while one was open for 0% of the time, Pallas kernels for 0%

commit v1 on v0

v1 whole, which is shorter than its diff:
```python
import jax
import jax.numpy as jnp
from jax import lax
from jax.experimental import pallas as pl
from jax.experimental.pallas import tpu as pltpu
from jax.sharding import PartitionSpec as P

MESH = pl.DeviceIdType.MESH
NX, NY, NZ = 4, 8, 8
ROWS, COLS = 192, 384
HALF = ROWS // 2
CUT = 80
SPAN = {1: ((0, 80), (0, 48), (48, 32)), 2: ((80, 112), (80, 64), (144, 48))}
GSPAN = ((0, 192), (0, 96), (96, 96))
N_SEMS = 160


def kernel(grad, basis, moment, second, update, moment_new, second_new, bp, gp, mom, sec, rot, dirn, own, give, got, chain_in, chain_out,
           local_sem, send_sem, recv_sem):
    row, col = lax.axis_index("row"), lax.axis_index("col")
    y, core = row // 2, row % 2
    z, x = col // NX, col % NX

    def at_x(d):
        return lax.rem(x + (d + NX), NX)

    def at_y(d):
        return lax.rem(y + (d + NY), NY)

    def at_z(d):
        return lax.rem(z + (d + NZ), NZ)

    def to_x(d):
        return {"row": row, "col": z * NX + at_x(d)}

    def to_y(d):
        return {"row": at_y(d) * 2 + core, "col": col}

    def to_z(d):
        return {"row": row, "col": at_z(d) * NX + x}

    sibling = {"row": y * 2 + 1 - core, "col": col}

    numbers = {}
    sent = []

    def number(key):
        return numbers.setdefault(key, len(numbers))

    def send(key, src, dst, device):
        k = number(key)
        copy = pltpu.make_async_remote_copy(
            src_ref=src, dst_ref=dst, send_sem=send_sem.at[k], recv_sem=recv_sem.at[k], device_id=device, device_id_type=MESH)
        copy.start()
        sent.append(copy)

    def arrive(key, dst):
        k = number(key)
        pltpu.make_async_remote_copy(
            src_ref=dst, dst_ref=dst, send_sem=send_sem.at[k], recv_sem=recv_sem.at[k], device_id=sibling, device_id_type=MESH).wait_recv()

    loads = [
        pltpu.make_async_copy(basis, bp.at[col], local_sem.at[0]),
        pltpu.make_async_copy(grad, gp.at[row], local_sem.at[1]),
        pltpu.make_async_copy(moment, mom, local_sem.at[2]),
        pltpu.make_async_copy(second, sec, local_sem.at[3]),
    ]
    for load in loads:
        load.start()

    barrier = pltpu.get_barrier_semaphore()
    for device in (to_x(1), to_x(-1), to_y(1), to_y(-1), to_z(1), to_z(-1), sibling):
        pl.semaphore_signal(barrier, inc=1, device_id=device, device_id_type=MESH)
    pl.semaphore_wait(barrier, 7)
    loads[0].wait()
    loads[1].wait()

    def piece(colour, dx, dz, part):
        start, size = SPAN[colour][part]
        return bp.at[at_z(dz) * NX + at_x(dx), pl.ds(start, size)]

    def flow(colour, axis, dx, dz, part, step):
        ref = piece(colour, dx, dz, part)
        if axis == "x":
            size, d = NX, dx - step
            key, device = ("b", colour, d if abs(d) < size // 2 else size // 2, dz, part), to_x(step)
        else:
            size, d = NZ, dz - step
            key, device = ("b", colour, dx, d if abs(d) < size // 2 else size // 2, part), to_z(step)
        send(key, ref, ref, device)

    def ring(colour, axis, dx, dz):
        d = dx if axis == "x" else dz
        far = (NX if axis == "x" else NZ) // 2
        other = dz if axis == "x" else dx
        plus, minus = (1, 2) if other % 2 == 0 else (2, 1)
        if d <= 0 and d > -far:
            flow(colour, axis, dx, dz, plus if d == 1 - far else 0, 1)
        if d >= 0 and d < far:
            flow(colour, axis, dx, dz, minus if d == far - 1 else 0, -1)

    def take(colour, dx, dz):
        far = (colour == 1 and dz == NZ // 2) or (colour == 2 and dx == NX // 2)
        if colour == 1:
            far = far or (dz == 0 and dx == NX // 2)
        else:
            far = far or (dx == 0 and dz == NZ // 2)
        for part in (1, 2) if far else (0,):
            arrive(("b", colour, dx, dz, part), piece(colour, dx, dz, part))

    def forward(colour, dx, dz):
        if colour == 1:
            if dz == 0:
                ring(1, "x", dx, 0)
            ring(1, "z", dx, dz)
        else:
            if dx == 0:
                ring(2, "z", 0, dz)
            ring(2, "x", dx, dz)

    def gblock(dy, part, c):
        start, size = GSPAN[part]
        return gp.at[at_y(dy) * 2 + c, pl.ds(start, size)]

    def share(dy):
        block = gblock(dy, 0, core)
        send(("s", dy), block, block, sibling)

    def gring(dy):
        far = NY // 2
        if dy <= 0 and dy > -far:
            d, part = dy - 1, 1 if dy == 1 - far else 0
            block = gblock(dy, part, core)
            send(("g", d if d > -far else far, part), block, block, to_y(1))
        if dy >= 0 and dy < far:
            d, part = dy + 1, 2 if dy == far - 1 else 0
            block = gblock(dy, part, core)
            send(("g", d, part), block, block, to_y(-1))

    def gtake(dy):
        for part in (1, 2) if dy == NY // 2 else (0,):
            arrive(("g", dy, part), gblock(dy, part, core))

    zs = [d for d in range(1 - NZ // 2, NZ // 2 + 1)]
    xs = [d for d in range(1 - NX // 2, NX // 2 + 1)]
    forward(1, 0, 0)
    forward(2, 0, 0)
    gring(0)
    share(0)
    for level in range(1, NX // 2 + NZ // 2 + 1):
        items = [(abs(dx) if colour == 2 else abs(dz), colour, dx, dz) for colour in (1, 2) for dx in xs for dz in zs
                 if abs(dx) + abs(dz) == level]
        for _, colour, dx, dz in sorted(items):
            take(colour, dx, dz)
            forward(colour, dx, dz)
        if level <= NY // 2:
            for dy in (-level, level) if level < NY // 2 else (level,):
                gtake(dy)
                gring(dy)
                share(dy)
    for dy in range(1 - NY // 2, NY // 2 + 1):
        arrive(("s", dy), gblock(dy, 0, 1 - core))

    def rotate(i, total):
        g = jnp.concatenate([gp[2 * i], gp[2 * i + 1]], axis=1)
        b = bp[pl.ds(4 * i, 4)].reshape(4 * ROWS, COLS)
        return total + jnp.dot(g, b, preferred_element_type=jnp.float32)

    rot[...] = lax.fori_loop(0, NZ, rotate, jnp.zeros((ROWS, COLS), jnp.float32))

    loads[2].wait()
    loads[3].wait()
    corr_one = 1.0 - 0.9**10
    corr_two = 1.0 - 0.95**10
    rotated = rot[...]
    m = 0.9 * mom[...] + 0.1 * rotated
    s = 0.95 * sec[...] + 0.05 * rotated * rotated
    mom[...] = m
    sec[...] = s
    dirn[...] = (m / corr_one / (jnp.sqrt(s / corr_two) + 1e-08)).astype(jnp.bfloat16)
    stores = [
        pltpu.make_async_copy(mom, moment_new, local_sem.at[4]),
        pltpu.make_async_copy(sec, second_new, local_sem.at[5]),
    ]
    for store in stores:
        store.start()

    def partial_block(dy, c):
        b = bp[pl.ds((at_y(dy) * 2 + c) * 2, 2)].reshape(2 * ROWS, COLS)
        return lax.dot_general(dirn[...], b, (((1,), (1,)), ((), ())), preferred_element_type=jnp.float32)

    order = [4, 3, -3, 2, -2, 1, -1, 0]
    for k, dy in enumerate(order):
        give[k] = partial_block(dy, 1 - core).astype(jnp.bfloat16)
        send(("p", k), give.at[k], got.at[k], sibling)
        own[k] = partial_block(dy, core)

    def chip_sum(k, h):
        return own[k, pl.ds(h * HALF, HALF)] + got[k, pl.ds(h * HALF, HALF)].astype(jnp.float32)

    def push(chain, distance, h):
        step = 1 - 2 * chain
        value = chip_sum(order.index(distance * step if distance < 4 else 4), h)
        first = distance == 4 or (distance == 3 and h != chain)
        slot = 2 * (distance - 1) + h
        if not first:
            arrive(("c", chain, distance, h), chain_in.at[chain, slot])
            value = value + chain_in[chain, slot].astype(jnp.float32)
        chain_out[chain, slot] = value.astype(jnp.bfloat16)
        dst = 2 * (distance - 2) + h if distance > 1 else 6 + h
        send(("c", chain, distance - 1, h), chain_out.at[chain, slot], chain_in.at[chain, dst], to_y(step))

    arrive(("p", 0), got.at[0])
    push(0, 4, 0)
    push(1, 4, 1)
    for distance in (3, 2, 1):
        for chain in (0, 1):
            arrive(("p", order.index(distance * (1 - 2 * chain))), got.at[order.index(distance * (1 - 2 * chain))])
        for first in (True, False):
            for chain in (0, 1):
                push(chain, distance, 1 - chain if first else chain)
    arrive(("p", 7), got.at[7])
    for h in (1, 0):
        value = chip_sum(7, h)
        for chain in (0, 1):
            arrive(("c", chain, 0, h), chain_in.at[chain, 6 + h])
            value = value + chain_in[chain, 6 + h].astype(jnp.float32)
        update[pl.ds(h * HALF, HALF)] = value.astype(jnp.bfloat16)
    for copy in sent:
        copy.wait_send()
    for store in stores:
        store.wait()


def per_device(grad, basis, moment, second):
    any_space = pl.BlockSpec(memory_space=pl.ANY)
    block = (ROWS, COLS)
    half = (HALF, COLS)
    return pl.pallas_call(
        kernel,
        out_shape=(
            jax.ShapeDtypeStruct(block, jnp.bfloat16),
            jax.ShapeDtypeStruct(block, jnp.float32),
            jax.ShapeDtypeStruct(block, jnp.float32),
        ),
        in_specs=[any_space] * 4,
        out_specs=(pl.BlockSpec(memory_space=pltpu.VMEM), any_space, any_space),
        scratch_shapes=[
            pltpu.VMEM((NX * NZ,) + block, jnp.bfloat16),
            pltpu.VMEM((2 * NY,) + block, jnp.bfloat16),
            pltpu.VMEM(block, jnp.float32),
            pltpu.VMEM(block, jnp.float32),
            pltpu.VMEM(block, jnp.float32),
            pltpu.VMEM(block, jnp.bfloat16),
            pltpu.VMEM((NY,) + block, jnp.float32),
            pltpu.VMEM((NY,) + block, jnp.bfloat16),
            pltpu.VMEM((NY,) + block, jnp.bfloat16),
            pltpu.VMEM((2, 8) + half, jnp.bfloat16),
            pltpu.VMEM((2, 8) + half, jnp.bfloat16),
            pltpu.SemaphoreType.DMA((6,)),
            pltpu.SemaphoreType.DMA((N_SEMS,)),
            pltpu.SemaphoreType.DMA((N_SEMS,)),
        ],
        compiler_params=pltpu.CompilerParams(collective_id=0, has_side_effects=True, vmem_limit_bytes=40 * 1024 * 1024),
        cost_estimate=pl.CostEstimate(flops=4 * 192 * 6144 * 384, bytes_accessed=2 * 10**6, transcendentals=ROWS * COLS),
    )(grad, basis, moment, second)


def solution(mesh):
    spec = P("col", "row")
    return jax.shard_map(
        per_device,
        mesh=mesh,
        in_specs=(spec,) * 4,
        out_specs=(spec,) * 3,
        check_vma=False,
    )
```

time: 227 us -> 75.1 us (0.33)
  waiting for transfers between devices: 202 us -> 0 us
  Pallas kernels: 0 us -> 68.4 us
  between operations: 13.8 us -> 0.65 us
  matrix products: 6.57 us -> 0 us
    all_gather x2 -> x0, waiting for transfers between devices: 139 us -> none  [the longest x1 90.5 us: per_device(): basis_panel = lax.all_gather(basis, 'col', axis=0, tiled=True)]
    pallas_call x0 -> x1, Pallas kernels: none -> 68.4 us  [per_device(): pl.pallas_call(kernel, out_shape=(jax.ShapeDtypeStruct(block, jnp.bfloat1...]
    unnamed x4 -> x0, waiting for transfers between devices: 63 us -> none
    dot_general x2 -> x0, matrix products: 6.57 us -> none  [the longest x1 4.7 us: per_device(): jnp.dot(grad_panel, basis_panel, preferred_element_type=jnp.float32)]
    unnamed x8 -> x11, local copies, waits for them, and re-layouts: 4.51 us -> 5.82 us
  transfers between devices with their start and end apart: 3 -> 0, of which waited for: 3 -> 0; matrix products, arithmetic and copies ran while one was open for 0% -> 0% of each run, Pallas kernels for 0% -> 0%
where the time goes in v1:
time: 75.1 us; the launch traced here: 74.9 us
  Pallas kernels  68.4 us (91%)
  local copies, waits for them, and re-layouts  5.82 us (8%)
    pallas_call x1, Pallas kernels, per_device(): pl.pallas_call(kernel, out_shape=(jax.ShapeDtypeStruct(block, jnp.bfloat1...  68.4 us
    unnamed x11, local copies, waits for them, and re-layouts  5.82 us

profile of v1, /device:TPU:6, one launch (start us, length us, event | category | flops | bytes accessed | tf_op | source)
XLA Modules:
  0.0 74.9 jit_solution(2373518336020709777)
XLA Ops:
  0.6 0.0 copy-start
  0.6 1.0 %copy-done = f32[192,384]{1,0:T(8,128)S(1)} copy-done((f32[192,384]{1,0:T(8,128)S(1)}, f32[192,384]{1,0:T(8,128)}, u32[]{:S(2)}) %copy-start) | copy-done | bytes 294936
  1.6 0.0 copy-start.1
  1.6 1.0 %copy-done.1 = f32[192,384]{1,0:T(8,128)S(1)} copy-done((f32[192,384]{1,0:T(8,128)S(1)}, f32[192,384]{1,0:T(8,128)}, u32[]{:S(2)}) %copy-start.1) | copy-done | bytes 294936
  2.6 0.0 copy-start.2
  2.6 0.9 %copy-done.2 = bf16[192,384]{1,0:T(8,128)(2,1)S(1)} copy-done((bf16[192,384]{1,0:T(8,128)(2,1)S(1)}, bf16[192,384]{1,0:T(8,128)(2,1)}, u32[]{:S(2)}) %copy-start.2) | copy-done | bytes 147480
  3.5 0.0 copy-start.3
  3.5 0.9 %copy-done.3 = bf16[192,384]{1,0:T(8,128)(2,1)S(1)} copy-done((bf16[192,384]{1,0:T(8,128)(2,1)S(1)}, bf16[192,384]{1,0:T(8,128)(2,1)}, u32[]{:S(2)}) %copy-start.3) | copy-done | bytes 147480
  4.4 68.4 %shard_map.67 = (bf16[192,384]{1,0:T(8,128)(2,1)S(1)}, f32[192,384]{1,0:T(8,128)S(1)}, f32[192,384]{1,0:T(8,128)S(1)}) custom-call(bf16[192,384]{1,0:T(8,128)(2,1)S(1)} %copy-done.2, bf16[192,384]{1,0:T(8,128)(2,1)S(1)} %copy-done.3, f32[192,384]{1,0:T(8,128)S(1)} %copy-done, f32[192,384]{1,0:T(8,128)S(1)} %copy-done.1), custom_call_target="tpu_custom_call" | custom-call | flops 1811939328 | bytes 2000000 | tf_op jit(solution)/shard_map/pallas_call | solution.py:239
  72.8 0.7 copy.10
  73.4 0.7 copy.11
  74.2 0.7 copy.12
Async XLA Ops:
  0.6 1.0 %copy-start = (f32[192,384]{1,0:T(8,128)S(1)}, f32[192,384]{1,0:T(8,128)}, u32[]{:S(2)}) copy-start(f32[192,384]{1,0:T(8,128)} %moment.1) | copy-start | bytes 884740
  1.6 1.0 %copy-start.1 = (f32[192,384]{1,0:T(8,128)S(1)}, f32[192,384]{1,0:T(8,128)}, u32[]{:S(2)}) copy-start(f32[192,384]{1,0:T(8,128)} %second.1) | copy-start | bytes 884740
  2.6 0.9 %copy-start.2 = (bf16[192,384]{1,0:T(8,128)(2,1)S(1)}, bf16[192,384]{1,0:T(8,128)(2,1)}, u32[]{:S(2)}) copy-start(bf16[192,384]{1,0:T(8,128)(2,1)} %grad.1) | copy-start | bytes 442372
  3.5 0.9 %copy-start.3 = (bf16[192,384]{1,0:T(8,128)(2,1)S(1)}, bf16[192,384]{1,0:T(8,128)(2,1)}, u32[]{:S(2)}) copy-start(bf16[192,384]{1,0:T(8,128)(2,1)} %basis.1) | copy-start | bytes 442372

commit v2 on v1

v2 whole, which is shorter than its diff:
```python
import jax
import jax.numpy as jnp
from jax import lax
from jax.experimental import pallas as pl
from jax.experimental.pallas import tpu as pltpu
from jax.sharding import PartitionSpec as P

MESH = pl.DeviceIdType.MESH
NX, NY, NZ = 4, 8, 8
ROWS, COLS = 192, 384
PARTS = 4
PART = ROWS // PARTS
COLOURS = (
    ("x", 0, 80, (48, 32), (0.5, 1.0, 0.0)),
    ("z", 80, 112, (64, 48), (1.0, 0.75, 0.0)),
)
GCUTS = 1
GHOP, GLAST = 0.95, 0.0
N_SEND, N_RECV = 48, 132


def kernel(grad, basis, moment, second, update, moment_new, second_new, bp, gp, mom, sec, rot, dirn, own, give, got, chain_in, chain_out,
           local_sem, send_sem, recv_sem):
    row, col = lax.axis_index("row"), lax.axis_index("col")
    y, core = row // 2, row % 2
    z, x = col // NX, col % NX

    def at_x(d):
        return lax.rem(x + (d + NX), NX)

    def at_y(d):
        return lax.rem(y + (d + NY), NY)

    def at_z(d):
        return lax.rem(z + (d + NZ), NZ)

    def to_x(d):
        return {"row": row, "col": z * NX + at_x(d)}

    def to_y(d):
        return {"row": at_y(d) * 2 + core, "col": col}

    def to_z(d):
        return {"row": row, "col": at_z(d) * NX + x}

    sibling = {"row": y * 2 + 1 - core, "col": col}

    numbers = {}
    sent = []

    def number(key):
        return numbers.setdefault(key, len(numbers))

    def send(key, src, dst, device):
        k = len(sent)
        if k >= N_SEND:
            sent[k - N_SEND].wait_send()
        copy = pltpu.make_async_remote_copy(
            src_ref=src, dst_ref=dst, send_sem=send_sem.at[k % N_SEND], recv_sem=recv_sem.at[number(key)], device_id=device,
            device_id_type=MESH)
        copy.start()
        sent.append(copy)

    def arrive(key, dst):
        pltpu.make_async_remote_copy(
            src_ref=dst, dst_ref=dst, send_sem=send_sem.at[0], recv_sem=recv_sem.at[number(key)], device_id=sibling,
            device_id_type=MESH).wait_recv()

    loads = [
        pltpu.make_async_copy(basis, bp.at[col], local_sem.at[0]),
        pltpu.make_async_copy(grad, gp.at[row], local_sem.at[1]),
        pltpu.make_async_copy(moment, mom, local_sem.at[2]),
        pltpu.make_async_copy(second, sec, local_sem.at[3]),
    ]
    for load in loads:
        load.start()

    barrier = pltpu.get_barrier_semaphore()
    for device in (to_x(1), to_x(-1), to_y(1), to_y(-1), to_z(1), to_z(-1), sibling):
        pl.semaphore_signal(barrier, inc=1, device_id=device, device_id_type=MESH)
    pl.semaphore_wait(barrier, 7)
    loads[0].wait()
    loads[1].wait()

    def piece(colour, dx, dz, part):
        _, start, size, parts, _ = COLOURS[colour]
        if part:
            start, size = start + (part - 1) * parts[0], parts[part - 1]
        return bp.at[at_z(dz) * NX + at_x(dx), pl.ds(start, size)]

    def ring(colour, axis, dx, dz):
        d, other, size, to = (dx, dz, NX, to_x) if axis == "x" else (dz, dx, NZ, to_z)
        far = size // 2
        parts = (1, 2) if (other + colour) % 2 == 0 else (2, 1)
        for step, part in zip((1, -1), parts):
            if (d if step == 1 else -d) in range(1 - far, 1):
                last = abs(d) == far - 1
                new = far if last else d - step
                part = part if last else 0
                ref = piece(colour, dx, dz, part)
                send(("b", colour, *((new, dz) if axis == "x" else (dx, new)), part), ref, ref, to(step))

    def take(colour, dx, dz):
        far_x, far_z = dx == NX // 2, dz == NZ // 2
        far = far_z or (far_x and dz == 0) if COLOURS[colour][0] == "x" else far_x or (far_z and dx == 0)
        for part in (1, 2) if far else (0,):
            arrive(("b", colour, dx, dz, part), piece(colour, dx, dz, part))

    def forward(colour, dx, dz):
        if COLOURS[colour][0] == "x":
            if dz == 0:
                ring(colour, "x", dx, 0)
            ring(colour, "z", dx, dz)
        else:
            if dx == 0:
                ring(colour, "z", 0, dz)
            ring(colour, "x", dx, dz)

    gsize = ROWS // GCUTS

    def gblock(dy, cut, part, c):
        start, size = (cut * gsize, gsize) if part == 0 else (cut * gsize + (part - 1) * gsize // 2, gsize // 2)
        return gp.at[at_y(dy) * 2 + c, pl.ds(start, size)]

    def gforward(dy, cut):
        far = NY // 2
        for step, part in ((1, 1), (-1, 2)):
            if (dy if step == 1 else -dy) in range(1 - far, 1):
                last = abs(dy) == far - 1
                block = gblock(dy, cut, part if last else 0, core)
                send(("g", far if last else dy - step, cut, part if last else 0), block, block, to_y(step))
        block = gblock(dy, cut, 0, core)
        send(("s", dy, cut), block, block, sibling)

    def gtake(dy, cut):
        for part in (1, 2) if dy == NY // 2 else (0,):
            arrive(("g", dy, cut, part), gblock(dy, cut, part, core))

    zs = [d for d in range(1 - NZ // 2, NZ // 2 + 1)]
    xs = [d for d in range(1 - NX // 2, NX // 2 + 1)]
    for colour in range(len(COLOURS)):
        forward(colour, 0, 0)
    for cut in range(GCUTS):
        gforward(0, cut)
    ys = range(1 - NY // 2, NY // 2 + 1)
    items = [(GHOP * abs(dy), -1, cut, dy, 0) for dy in ys for cut in range(GCUTS) if dy]
    items.append((GHOP * NY / 2 + GLAST, 9, 0, 0, 0))
    for colour, (first, _, _, _, (wx, wz, offset)) in enumerate(COLOURS):
        items += [(offset + wx * abs(dx) + wz * abs(dz), colour, abs(dx if first == "z" else dz), dx, dz) for dx in xs for dz in zs if dx or dz]
    missing = {dz: len(COLOURS) * (NX - (dz == 0)) for dz in zs}
    ready = []
    gathered = False

    def rotate(dz):
        k = at_z(dz)
        g = jnp.concatenate([gp[2 * k], gp[2 * k + 1]], axis=1)
        b = bp[pl.ds(4 * k, 4)].reshape(4 * ROWS, COLS)
        rot[...] += jnp.dot(g, b, preferred_element_type=jnp.float32)

    rot[...] = jnp.zeros_like(rot)
    for _, colour, cut, dx, dz in sorted(items):
        if colour == -1:
            gtake(dx, cut)
            gforward(dx, cut)
        elif colour == 9:
            for dy in ys:
                for cut in range(GCUTS):
                    arrive(("s", dy, cut), gblock(dy, cut, 0, 1 - core))
            gathered = True
        else:
            take(colour, dx, dz)
            forward(colour, dx, dz)
            missing[dz] -= 1
            if missing[dz] == 0:
                ready.append(dz)
            if gathered and ready:
                rotate(ready.pop(0))
    for dz in ready:
        rotate(dz)

    loads[2].wait()
    loads[3].wait()
    def partial_block(dy, c, rows=slice(None)):
        b = bp[pl.ds((at_y(dy) * 2 + c) * 2, 2)].reshape(2 * ROWS, COLS)
        return lax.dot_general(dirn[rows], b, (((1,), (1,)), ((), ())), preferred_element_type=jnp.float32)

    order = [4, 3, -3, 2, -2, 1, -1, 0]
    corr_one = 1.0 - 0.9**10
    corr_two = 1.0 - 0.95**10

    def direct(h):
        rows = pl.ds(h * PART, PART)
        rotated = rot[rows]
        m = 0.9 * mom[rows] + 0.1 * rotated
        s = 0.95 * sec[rows] + 0.05 * rotated * rotated
        moment_new[rows] = m
        second_new[rows] = s
        dirn[rows] = (m / corr_one / (jnp.sqrt(s / corr_two) + 1e-08)).astype(jnp.bfloat16)

    def give_block(k):
        give[k] = partial_block(order[k], 1 - core).astype(jnp.bfloat16)
        send(("p", k), give.at[k], got.at[k], sibling)

    def own_block(k):
        own[k] = partial_block(order[k], core)

    def chip_sum(k, h):
        return own[k, pl.ds(h * PART, PART)] + got[k, pl.ds(h * PART, PART)].astype(jnp.float32)

    def push(chain, distance, h):
        step = 1 - 2 * chain
        value = chip_sum(order.index(distance * step if distance < 4 else 4), h)
        slot = PARTS * (distance - 1) + h
        if distance < 3 or (distance == 3 and h in early[chain]):
            arrive(("c", chain, distance, h), chain_in.at[chain, slot])
            value = value + chain_in[chain, slot].astype(jnp.float32)
        chain_out[chain, slot] = value.astype(jnp.bfloat16)
        dst = PARTS * (distance - 2) + h if distance > 1 else 3 * PARTS + h
        send(("c", chain, distance - 1, h), chain_out.at[chain, slot], chain_in.at[chain, dst], to_y(step))

    early = (range(PARTS // 2), range(PARTS // 2, PARTS))
    starts = [early[c][i] for i in range(PARTS // 2) for c in (0, 1)]
    for h in starts:
        direct(h)
        rows = pl.ds(h * PART, PART)
        give[0, rows] = partial_block(order[0], 1 - core, rows).astype(jnp.bfloat16)
        send(("p", 0, h), give.at[0, rows], got.at[0, rows], sibling)
    give_block(1)
    give_block(2)
    own_block(0)
    for h in starts:
        arrive(("p", 0, h), got.at[0, pl.ds(h * PART, PART)])
        push(0 if h in early[0] else 1, 4, h)
    own_block(1)
    own_block(2)
    for distance in (3, 2, 1):
        for chain in (0, 1):
            k = order.index(distance * (1 - 2 * chain))
            arrive(("p", k), got.at[k])
        for first in (True, False):
            for h in range(PARTS // 2):
                push(0, distance, early[1 if first else 0][h])
                push(1, distance, early[0 if first else 1][h])
            if distance == 3 and first:
                for k in range(3, 8):
                    give_block(k)
                for k in range(3, 8):
                    own_block(k)
    arrive(("p", 7), got.at[7])
    for h in [early[1 - c][i] for i in range(PARTS // 2) for c in (0, 1)]:
        value = chip_sum(7, h)
        for chain in (0, 1):
            arrive(("c", chain, 0, h), chain_in.at[chain, 3 * PARTS + h])
            value = value + chain_in[chain, 3 * PARTS + h].astype(jnp.float32)
        update[pl.ds(h * PART, PART)] = value.astype(jnp.bfloat16)
    for copy in sent[-N_SEND:]:
        copy.wait_send()


def finish(*refs):
    copies = [pltpu.make_async_copy(refs[i], refs[3 + i], refs[6].at[i]) for i in range(3)]
    for copy in copies:
        copy.start()
    for copy in copies:
        copy.wait()


def per_device(grad, basis, moment, second):
    any_space = pl.BlockSpec(memory_space=pl.ANY)
    block = (ROWS, COLS)
    results = pl.pallas_call(
        kernel,
        out_shape=(
            pltpu.VMEM(block, jnp.bfloat16),
            pltpu.VMEM(block, jnp.float32),
            pltpu.VMEM(block, jnp.float32),
        ),
        in_specs=[any_space] * 4,
        out_specs=(pl.BlockSpec(memory_space=pltpu.VMEM),) * 3,
        scratch_shapes=[
            pltpu.VMEM((NX * NZ,) + block, jnp.bfloat16),
            pltpu.VMEM((2 * NY,) + block, jnp.bfloat16),
            pltpu.VMEM(block, jnp.float32),
            pltpu.VMEM(block, jnp.float32),
            pltpu.VMEM(block, jnp.float32),
            pltpu.VMEM(block, jnp.bfloat16),
            pltpu.VMEM((NY,) + block, jnp.float32),
            pltpu.VMEM((NY,) + block, jnp.bfloat16),
            pltpu.VMEM((NY,) + block, jnp.bfloat16),
            pltpu.VMEM((2, 4 * PARTS, PART, COLS), jnp.bfloat16),
            pltpu.VMEM((2, 4 * PARTS, PART, COLS), jnp.bfloat16),
            pltpu.SemaphoreType.DMA((4,)),
            pltpu.SemaphoreType.DMA((N_SEND,)),
            pltpu.SemaphoreType.DMA((N_RECV,)),
        ],
        compiler_params=pltpu.CompilerParams(collective_id=0, has_side_effects=True, vmem_limit_bytes=58 * 1024 * 1024),
        cost_estimate=pl.CostEstimate(flops=4 * 192 * 6144 * 384, bytes_accessed=2 * 10**6, transcendentals=ROWS * COLS),
    )(grad, basis, moment, second)
    return results


def solution(mesh):
    spec = P("col", "row")
    return jax.shard_map(
        per_device,
        mesh=mesh,
        in_specs=(spec,) * 4,
        out_specs=(spec,) * 3,
        check_vma=False,
    )
```

time: 75.1 us -> 64.8 us (0.86)
  Pallas kernels: 68.4 us -> 61.1 us
  local copies, waits for them, and re-layouts: 5.82 us -> 2.09 us
    pallas_call x1, Pallas kernels: 68.4 us -> 61.1 us  [per_device(): pl.pallas_call(kernel, out_shape=(pltpu.VMEM(block, jnp.bfloat16), pltpu....]
    unnamed x11 -> x3, local copies, waits for them, and re-layouts: 5.82 us -> 2.09 us
where the time goes in v2:
time: 64.8 us; the launch traced here: 63.9 us
  Pallas kernels  61.1 us (94%)
  local copies, waits for them, and re-layouts  2.09 us (3%)
    pallas_call x1, Pallas kernels, per_device(): pl.pallas_call(kernel, out_shape=(pltpu.VMEM(block, jnp.bfloat16), pltpu....  61.1 us
    unnamed x3, local copies, waits for them, and re-layouts  2.09 us

profile of v2, /device:TPU:6, one launch (start us, length us, event | category | flops | bytes accessed | tf_op | source)
XLA Modules:
  0.0 63.9 jit_solution(1544530132860547946)
XLA Ops:
  0.6 61.1 %shard_map.67 = (bf16[192,384]{1,0:T(8,128)(2,1)S(1)}, f32[192,384]{1,0:T(8,128)S(1)}, f32[192,384]{1,0:T(8,128)S(1)}) custom-call(bf16[192,384]{1,0:T(8,128)(2,1)} %grad.1, bf16[192,384]{1,0:T(8,128)(2,1)} %basis.1, f32[192,384]{1,0:T(8,128)} %moment.1, f32[192,384]{1,0:T(8,128)} %second.1), custom_call_target="tpu_custom_call" | custom-call | flops 1811939328 | bytes 2000000 | tf_op jit(solution)/shard_map/pallas_call | solution.py:271
  61.8 0.7 %copy.10 = bf16[192,384]{1,0:T(8,128)(2,1)} copy(bf16[192,384]{1,0:T(8,128)(2,1)S(1)} %get-tuple-element.3) | data formatting | bytes 294912
  62.4 0.7 %copy.11 = f32[192,384]{1,0:T(8,128)} copy(f32[192,384]{1,0:T(8,128)S(1)} %get-tuple-element.4) | data formatting | bytes 589824
  63.1 0.7 %copy.12 = f32[192,384]{1,0:T(8,128)} copy(f32[192,384]{1,0:T(8,128)S(1)} %get-tuple-element.5) | data formatting | bytes 589824

commit v3 on v2

v3 whole, which is shorter than its diff:
```python
import functools

import jax
import jax.numpy as jnp
from jax import lax
from jax.experimental import pallas as pl
from jax.experimental.pallas import tpu as pltpu
from jax.sharding import PartitionSpec as P

MESH = pl.DeviceIdType.MESH
NX, NY, NZ = 4, 8, 8
ROWS, COLS = 192, 384
PARTS = 4
PART = ROWS // PARTS
COLOURS = (
    ("x", 0, 80, (48, 32)),
    ("z", 80, 112, (64, 48)),
)
GCUTS = 2
N_SEND, N_PUSH, N_RECV = 40, 24, 132

SPLIT = (4, 4, 4, 4, 3, 4, 4, 4)
ORDERS = (
    (80, 3, 81, 44, 69, 19, 12, 51, 10, 35, 42, 27, 36, 45, 73, 20, 72, 68, 2, 34, 50, 18, 21, 41, 53, 75, 28, 67, 9, 46, 17, 74, 52,
     4, 66, 40, 26, 77, 65, 5, 47, 33, 25, 38, 76, 22, 64, 49, 1, 13, 8, 37, 32, 29, 79, 54, 78, 39, 48, 0, 55, 58, 15, 24, 57, 30, 7,
     82, 59, 16, 61, 14, 23, 6, 62, 56, 60, 31, 63),
    (80, 3, 19, 12, 72, 69, 44, 10, 51, 27, 42, 73, 68, 20, 2, 67, 4, 45, 13, 74, 18, 41, 66, 52, 75, 36, 21, 1, 65, 37, 46, 26, 64,
     35, 29, 28, 40, 33, 6, 77, 17, 60, 49, 14, 76, 54, 9, 8, 47, 38, 22, 59, 34, 25, 16, 48, 53, 32, 5, 78, 57, 50, 79, 30, 24, 82,
     39, 55, 0, 15, 58, 61, 56, 62, 7, 31, 63, 23),
    (80, 3, 72, 12, 19, 42, 73, 69, 44, 27, 68, 2, 20, 75, 74, 35, 9, 45, 36, 34, 18, 66, 41, 28, 5, 51, 17, 52, 76, 13, 77, 67, 10,
     26, 64, 46, 40, 50, 21, 4, 25, 29, 65, 60, 0, 49, 47, 1, 6, 33, 14, 58, 38, 78, 37, 53, 16, 79, 54, 22, 8, 39, 48, 32, 30, 82, 55,
     24, 59, 31, 61, 7, 57, 23, 15, 62, 63, 56),
    (80, 3, 19, 69, 68, 42, 44, 73, 72, 35, 27, 10, 4, 12, 41, 51, 67, 45, 50, 34, 75, 66, 20, 13, 18, 1, 33, 52, 65, 28, 74, 26, 2,
     36, 37, 59, 77, 46, 5, 21, 40, 17, 49, 29, 25, 9, 47, 8, 76, 60, 64, 38, 16, 53, 22, 6, 32, 54, 0, 30, 48, 78, 55, 39, 24, 79, 14,
     7, 82, 57, 61, 56, 58, 23, 62, 63, 31, 15),
    (80, 3, 19, 68, 44, 12, 42, 66, 20, 72, 69, 27, 41, 18, 45, 34, 73, 50, 26, 52, 9, 4, 40, 28, 46, 2, 21, 67, 51, 75, 64, 5, 33, 74,
     10, 25, 35, 36, 29, 1, 53, 47, 32, 13, 65, 17, 49, 0, 6, 77, 16, 37, 76, 48, 60, 59, 24, 38, 30, 54, 22, 14, 39, 8, 79, 55, 78,
     82, 7, 56, 15, 62, 61, 57, 58, 31, 63, 23),
    (80, 3, 19, 44, 69, 12, 72, 42, 68, 20, 35, 73, 27, 10, 67, 36, 45, 4, 75, 66, 41, 74, 50, 21, 40, 2, 52, 18, 28, 46, 17, 64, 49,
     33, 34, 5, 77, 37, 26, 65, 76, 29, 47, 1, 13, 79, 51, 9, 54, 78, 25, 60, 8, 53, 48, 32, 6, 38, 14, 0, 55, 24, 30, 58, 82, 39, 16,
     22, 61, 56, 23, 62, 31, 7, 57, 59, 15, 63),
    (80, 19, 3, 72, 44, 68, 42, 74, 27, 20, 4, 35, 10, 41, 69, 52, 73, 36, 66, 45, 51, 18, 12, 2, 67, 28, 26, 46, 33, 75, 40, 49, 5,
     64, 60, 13, 29, 76, 65, 21, 47, 34, 37, 53, 77, 9, 1, 16, 78, 14, 54, 38, 50, 48, 59, 0, 79, 30, 22, 17, 6, 32, 82, 39, 55, 25,
     61, 24, 58, 57, 8, 23, 15, 63, 7, 62, 56, 31),
    (3, 19, 68, 69, 73, 72, 12, 42, 44, 10, 18, 45, 41, 27, 67, 66, 4, 26, 36, 20, 2, 9, 50, 28, 46, 34, 64, 13, 74, 37, 52, 53, 49,
     75, 1, 25, 17, 29, 47, 21, 54, 5, 76, 61, 77, 60, 65, 35, 40, 39, 33, 55, 6, 58, 38, 22, 78, 14, 51, 79, 30, 48, 82, 32, 0, 57,
     23, 62, 31, 7, 59, 15, 8, 16, 56, 63, 24),
)


def kernel(grad, basis, moment, second, update, rot, bp, gp, mom, sec, dirn, own, give, got, chain_in, chain_out,
           local_sem, send_sem, push_sem, recv_sem, ready_sem):
    row, col = lax.axis_index("row"), lax.axis_index("col")
    y, core = row // 2, row % 2
    z, x = col // NX, col % NX

    def at_x(d):
        return lax.rem(x + (d + NX), NX)

    def at_y(d):
        return lax.rem(y + (d + NY), NY)

    def at_z(d):
        return lax.rem(z + (d + NZ), NZ)

    def to_x(d):
        return {"row": row, "col": z * NX + at_x(d)}

    def to_y(d):
        return {"row": at_y(d) * 2 + core, "col": col}

    def to_z(d):
        return {"row": row, "col": at_z(d) * NX + x}

    sibling = {"row": y * 2 + 1 - core, "col": col}

    def to_sibling():
        return sibling

    numbers = {}

    def number(key):
        return numbers.setdefault(key, len(numbers))

    class Outbox(list):
        def __init__(self, sem, size):
            super().__init__()
            self.sem, self.size = sem, size

        def send(self, key, ref, device, dst=None):
            k, n = len(self), number(key)
            if k >= self.size:
                self[k - self.size]().wait_send()

            def copy():
                return pltpu.make_async_remote_copy(
                    src_ref=ref(), dst_ref=(dst or ref)(), send_sem=self.sem.at[k % self.size], recv_sem=recv_sem.at[n],
                    device_id=device(), device_id_type=MESH)

            copy().start()
            self.append(copy)

        def drain(self):
            for copy in self[-self.size:]:
                copy().wait_send()

    def arrive(key, dst):
        pltpu.make_async_remote_copy(
            src_ref=dst, dst_ref=dst, send_sem=send_sem.at[0], recv_sem=recv_sem.at[number(key)], device_id=sibling,
            device_id_type=MESH).wait_recv()

    loads = [
        pltpu.make_async_copy(basis, bp.at[col], local_sem.at[0]),
        pltpu.make_async_copy(grad, gp.at[row], local_sem.at[1]),
        pltpu.make_async_copy(moment, mom, local_sem.at[2]),
        pltpu.make_async_copy(second, sec, local_sem.at[3]),
    ]
    for load in loads:
        load.start()

    barrier = pltpu.get_barrier_semaphore()
    for device in (to_x(1), to_x(-1), to_y(1), to_y(-1), sibling):
        pl.semaphore_signal(barrier, inc=1, device_id=device, device_id_type=MESH)

    @pl.when(z < NZ - 1)
    def _():
        pl.semaphore_signal(barrier, inc=1, device_id=to_z(1), device_id_type=MESH)

    @pl.when(z == 0)
    def _():
        pl.semaphore_signal(barrier, inc=1, device_id=to_z(-1), device_id_type=MESH)

    pl.semaphore_wait(barrier, 5 + jnp.where(z > 0, 1, 0) + jnp.where(z == NZ - 1, 1, 0))

    @pl.when(z > 0)
    def _():
        pl.semaphore_signal(ready_sem.at[0], inc=1, device_id=to_z(-1), device_id_type=MESH)

    @pl.when(z == NZ - 1)
    def _():
        pl.semaphore_signal(ready_sem.at[1], inc=1, device_id=to_z(1), device_id_type=MESH)

    loads[0].wait()
    loads[1].wait()

    def piece(here, colour, dx, dz, part):
        _, start, size, parts = COLOURS[colour]
        if part:
            start, size = start + (part - 1) * parts[0], parts[part - 1]
        return bp.at[(here + dz) % NZ * NX + at_x(dx), pl.ds(start, size)]

    def ring(send, here, colour, axis, dx, dz):
        d, other, size, to = (dx, dz, NX, to_x) if axis == "x" else (dz, dx, NZ, to_z)
        far = size // 2
        parts = (1, 2) if (other + colour) % 2 == 0 else (2, 1)
        for step, part in zip((1, -1), parts):
            if axis == "x":
                if (d if step == 1 else -d) not in range(1 - far, 1):
                    continue
                last = abs(d) == far - 1
                key = ("b", colour, far if last else d - step, -dz % NZ)
            else:
                hops, split = -dz % NZ, SPLIT[(here + dz) % NZ]
                new = (hops + step) % NZ
                if hops and (hops >= split if step == 1 else hops <= split):
                    continue
                last = new == split
                key = ("b", colour, dx, new)
            send(step if axis == "z" else 0, key, functools.partial(piece, here, colour, dx, dz, part if last else 0),
                 functools.partial(to, step))

    def forward(send, here, colour, dx, dz):
        if COLOURS[colour][0] == "x":
            if dz == 0:
                ring(send, here, colour, "x", dx, 0)
            ring(send, here, colour, "z", dx, dz)
        else:
            if dx == 0:
                ring(send, here, colour, "z", 0, dz)
            ring(send, here, colour, "x", dx, dz)

    gsize = ROWS // GCUTS

    def gblock(dy, cut, part, c):
        start, size = (cut * gsize, gsize) if part == 0 else (cut * gsize + (part - 1) * gsize // 2, gsize // 2)
        return gp.at[at_y(dy) * 2 + c, pl.ds(start, size)]

    def gforward(box, dy, cut):
        far = NY // 2
        for step, part in ((1, 1), (-1, 2)):
            if (dy if step == 1 else -dy) in range(1 - far, 1):
                last = abs(dy) == far - 1
                box.send(("g", far if last else dy - step, cut), functools.partial(gblock, dy, cut, part if last else 0, core),
                         functools.partial(to_y, step))
        box.send(("s", dy, cut), functools.partial(gblock, dy, cut, 0, core), to_sibling)

    def rotate(k):
        g = jnp.concatenate([gp[2 * k], gp[2 * k + 1]], axis=1)
        b = bp[pl.ds(4 * k, 4)].reshape(4 * ROWS, COLS)
        rot[...] += jnp.dot(g, b, preferred_element_type=jnp.float32)

    rot[...] = jnp.zeros_like(rot)

    def gather(here, box):
        waiting = {1: [], -1: []}
        if here == NZ - 1:
            waiting[1] = None
        if here > 0:
            waiting[-1] = None

        def send(step, *copy):
            if step and waiting[step] is not None:
                waiting[step].append(copy)
            else:
                box.send(*copy)

        missing = [2 * NX - 2 * (k == here) for k in range(NZ)]
        ready = []
        gathered = False
        for colour in (0, 1):
            forward(send, here, colour, 0, 0)
        for cut in range(GCUTS):
            gforward(box, 0, cut)
        for item in ORDERS[here]:
            if item in (80, 81):
                pl.semaphore_wait(ready_sem.at[item - 80], 1)
                step = 161 - 2 * item
                for copy in waiting[step]:
                    box.send(*copy)
                waiting[step] = None
            elif item == 82:
                for dy in range(1 - NY // 2, NY // 2 + 1):
                    for cut in range(GCUTS):
                        arrive(("s", dy, cut), gblock(dy, cut, 0, 1 - core))
                gathered = True
            elif item >= 64:
                dy, cut = (item - 64) // 2 - 3, item % 2
                arrive(("g", dy, cut), gblock(dy, cut, 0, core))
                gforward(box, dy, cut)
            else:
                colour, dx, dz = item // 32, item % 32 // 8 - 1, item % 8 - 3
                arrive(("b", colour, dx, -dz % NZ), piece(here, colour, dx, dz, 0))
                forward(send, here, colour, dx, dz)
                k = (here + dz) % NZ
                missing[k] -= 1
                if missing[k] == 0:
                    ready.append(k)
                if gathered and ready:
                    rotate(ready.pop(0))
        for k in ready:
            rotate(k)

    boxes = [Outbox(send_sem, N_SEND) for _ in range(NZ)]
    for here in range(NZ):
        pl.when(z == here)(functools.partial(gather, here, boxes[here]))

    loads[2].wait()
    loads[3].wait()
    def partial_block(dy, c, rows=slice(None)):
        b = bp[pl.ds((at_y(dy) * 2 + c) * 2, 2)].reshape(2 * ROWS, COLS)
        return lax.dot_general(dirn[rows], b, (((1,), (1,)), ((), ())), preferred_element_type=jnp.float32)

    pushed = Outbox(push_sem, N_PUSH)
    order = [4, 3, -3, 2, -2, 1, -1, 0]
    corr_one = 1.0 - 0.9**10
    corr_two = 1.0 - 0.95**10

    def direct(h):
        rows = pl.ds(h * PART, PART)
        rotated = rot[rows]
        m, s = moments(mom[rows], sec[rows], rotated)
        dirn[rows] = (m / corr_one / (jnp.sqrt(s / corr_two) + 1e-08)).astype(jnp.bfloat16)

    def give_block(k):
        give[k] = partial_block(order[k], 1 - core).astype(jnp.bfloat16)
        pushed.send(("p", k), lambda: give.at[k], to_sibling, lambda: got.at[k])

    def own_block(k):
        own[k] = partial_block(order[k], core)

    def chip_sum(k, h):
        return own[k, pl.ds(h * PART, PART)] + got[k, pl.ds(h * PART, PART)].astype(jnp.float32)

    def push(chain, distance, h):
        step = 1 - 2 * chain
        value = chip_sum(order.index(distance * step if distance < 4 else 4), h)
        slot = PARTS * (distance - 1) + h
        if distance < 3 or (distance == 3 and h in early[chain]):
            arrive(("c", chain, distance, h), chain_in.at[chain, slot])
            value = value + chain_in[chain, slot].astype(jnp.float32)
        chain_out[chain, slot] = value.astype(jnp.bfloat16)
        dst = PARTS * (distance - 2) + h if distance > 1 else 3 * PARTS + h
        pushed.send(("c", chain, distance - 1, h), lambda: chain_out.at[chain, slot], functools.partial(to_y, step),
                    lambda: chain_in.at[chain, dst])

    early = (range(PARTS // 2), range(PARTS // 2, PARTS))
    starts = [early[c][i] for i in range(PARTS // 2) for c in (0, 1)]
    for h in starts:
        direct(h)
        rows = pl.ds(h * PART, PART)
        give[0, rows] = partial_block(order[0], 1 - core, rows).astype(jnp.bfloat16)
        pushed.send(("p", 0, h), functools.partial(lambda r: give.at[0, r], rows), to_sibling, functools.partial(lambda r: got.at[0, r], rows))
    give_block(1)
    give_block(2)
    own_block(0)
    for h in starts:
        arrive(("p", 0, h), got.at[0, pl.ds(h * PART, PART)])
        push(0 if h in early[0] else 1, 4, h)
    own_block(1)
    own_block(2)
    for distance in (3, 2, 1):
        for chain in (0, 1):
            k = order.index(distance * (1 - 2 * chain))
            arrive(("p", k), got.at[k])
        for first in (True, False):
            for h in range(PARTS // 2):
                push(0, distance, early[1 if first else 0][h])
                push(1, distance, early[0 if first else 1][h])
            if distance == 3 and first:
                for k in range(3, 8):
                    give_block(k)
                for k in range(3, 8):
                    own_block(k)
    arrive(("p", 7), got.at[7])
    for h in [early[1 - c][i] for i in range(PARTS // 2) for c in (0, 1)]:
        value = chip_sum(7, h)
        for chain in (0, 1):
            arrive(("c", chain, 0, h), chain_in.at[chain, 3 * PARTS + h])
            value = value + chain_in[chain, 3 * PARTS + h].astype(jnp.float32)
        update[pl.ds(h * PART, PART)] = value.astype(jnp.bfloat16)
    for here in range(NZ):
        pl.when(z == here)(boxes[here].drain)
    pushed.drain()


def moments(moment, second, rotated):
    return 0.9 * moment + 0.1 * rotated, 0.95 * second + 0.05 * rotated * rotated


def per_device(grad, basis, moment, second):
    any_space = pl.BlockSpec(memory_space=pl.ANY)
    block = (ROWS, COLS)
    update, rotated = pl.pallas_call(
        kernel,
        out_shape=(
            pltpu.VMEM(block, jnp.bfloat16),
            pltpu.VMEM(block, jnp.float32),
        ),
        in_specs=[any_space] * 4,
        out_specs=(pl.BlockSpec(memory_space=pltpu.VMEM),) * 2,
        scratch_shapes=[
            pltpu.VMEM((NX * NZ,) + block, jnp.bfloat16),
            pltpu.VMEM((2 * NY,) + block, jnp.bfloat16),
            pltpu.VMEM(block, jnp.float32),
            pltpu.VMEM(block, jnp.float32),
            pltpu.VMEM(block, jnp.bfloat16),
            pltpu.VMEM((NY,) + block, jnp.float32),
            pltpu.VMEM((NY,) + block, jnp.bfloat16),
            pltpu.VMEM((NY,) + block, jnp.bfloat16),
            pltpu.VMEM((2, 4 * PARTS, PART, COLS), jnp.bfloat16),
            pltpu.VMEM((2, 4 * PARTS, PART, COLS), jnp.bfloat16),
            pltpu.SemaphoreType.DMA((4,)),
            pltpu.SemaphoreType.DMA((N_SEND,)),
            pltpu.SemaphoreType.DMA((N_PUSH,)),
            pltpu.SemaphoreType.DMA((N_RECV,)),
            pltpu.SemaphoreType.REGULAR((2,)),
        ],
        compiler_params=pltpu.CompilerParams(collective_id=0, has_side_effects=True, vmem_limit_bytes=58 * 1024 * 1024),
        cost_estimate=pl.CostEstimate(flops=4 * 192 * 6144 * 384, bytes_accessed=2 * 10**6, transcendentals=ROWS * COLS),
    )(grad, basis, moment, second)
    return (update, *moments(moment, second, rotated))


def solution(mesh):
    spec = P("col", "row")
    return jax.shard_map(
        per_device,
        mesh=mesh,
        in_specs=(spec,) * 4,
        out_specs=(spec,) * 3,
        check_vma=False,
    )
```

time: 64.8 us -> 62.1 us (0.958)
  Pallas kernels: 61.1 us -> 58.5 us
  local copies, waits for them, and re-layouts: 2.09 us -> 1.01 us
  other arithmetic: 0 us -> 0.9 us
    pallas_call x1, Pallas kernels: 61.1 us -> 58.5 us  [per_device(): pl.pallas_call(kernel, out_shape=(pltpu.VMEM(block, jnp.bfloat16), pltpu....]
    unnamed x3 -> x5, local copies, waits for them, and re-layouts: 2.09 us -> 1.01 us
    add x0 -> x1, other arithmetic: none -> 0.9 us  [moments(): 0.95 * second + 0.05 * rotated * rotated]
where the time goes in v3:
time: 62.1 us; the launch traced here: 61 us
  Pallas kernels  58.5 us (94%)
  local copies, waits for them, and re-layouts  1.01 us (2%)
  other arithmetic  0.9 us (1%)
  between operations  0.66 us (1%)
    pallas_call x1, Pallas kernels, per_device(): pl.pallas_call(kernel, out_shape=(pltpu.VMEM(block, jnp.bfloat16), pltpu....  58.5 us

profile of v3, /device:TPU:6, one launch (start us, length us, event | category | flops | bytes accessed | tf_op | source)
XLA Modules:
  0.0 61.0 jit_solution(7116232688343069496)
XLA Ops:
  0.6 0.0 copy-start.1
  0.6 58.5 %shard_map.67 = (bf16[192,384]{1,0:T(8,128)(2,1)S(1)}, f32[192,384]{1,0:T(8,128)S(1)}) custom-call(bf16[192,384]{1,0:T(8,128)(2,1)} %grad.1, bf16[192,384]{1,0:T(8,128)(2,1)} %basis.1, f32[192,384]{1,0:T(8,128)} %moment.1, f32[192,384]{1,0:T(8,128)} %second.1), custom_call_target="tpu_custom_call" | custom-call | flops 1811939328 | bytes 2000000 | tf_op jit(solution)/shard_map/pallas_call | solution.py:343
  59.1 0.0 copy-start
  59.1 0.7 %copy.8 = bf16[192,384]{1,0:T(8,128)(2,1)} copy(bf16[192,384]{1,0:T(8,128)(2,1)S(1)} %get-tuple-element.9) | data formatting | bytes 294912
  59.8 0.0 copy-done.1
  59.8 0.3 copy-done
  60.1 0.9 %fusion = (f32[192,384]{1,0:T(8,128)}, f32[192,384]{1,0:T(8,128)}) fusion(f32[192,384]{1,0:T(8,128)S(1)} %get-tuple-element.6, f32[192,384]{1,0:T(8,128)S(1)} %copy-done.1, f32[192,384]{1,0:T(8,128)S(1)} %copy-done), kind=kLoop, calls=%fused_computation.1 | loop fusion | flops 516096 | bytes 1474560 | tf_op jit(solution)/shard_map/add | solution.py:337
Async XLA Ops:
  0.6 59.2 %copy-start.1 = (f32[192,384]{1,0:T(8,128)S(1)}, f32[192,384]{1,0:T(8,128)}, u32[]{:S(2)}) copy-start(f32[192,384]{1,0:T(8,128)} %second.1) | copy-start | bytes 884740
  59.1 1.0 %copy-start = (f32[192,384]{1,0:T(8,128)S(1)}, f32[192,384]{1,0:T(8,128)}, u32[]{:S(2)}) copy-start(f32[192,384]{1,0:T(8,128)} %moment.1) | copy-start | bytes 884740

commit v4 on v3

--- a/solution.py
+++ b/solution.py
@@ -17,34 +17,34 @@
     ("z", 80, 112, (64, 48)),
 )
 GCUTS = 2
-N_SEND, N_PUSH, N_RECV = 40, 24, 132
+N_SEND, N_PUSH, N_RECV = 28, 16, 116
 
 SPLIT = (4, 4, 4, 4, 3, 4, 4, 4)
 ORDERS = (
-    (80, 3, 81, 44, 69, 19, 12, 51, 10, 35, 42, 27, 36, 45, 73, 20, 72, 68, 2, 34, 50, 18, 21, 41, 53, 75, 28, 67, 9, 46, 17, 74, 52,
-     4, 66, 40, 26, 77, 65, 5, 47, 33, 25, 38, 76, 22, 64, 49, 1, 13, 8, 37, 32, 29, 79, 54, 78, 39, 48, 0, 55, 58, 15, 24, 57, 30, 7,
-     82, 59, 16, 61, 14, 23, 6, 62, 56, 60, 31, 63),
-    (80, 3, 19, 12, 72, 69, 44, 10, 51, 27, 42, 73, 68, 20, 2, 67, 4, 45, 13, 74, 18, 41, 66, 52, 75, 36, 21, 1, 65, 37, 46, 26, 64,
-     35, 29, 28, 40, 33, 6, 77, 17, 60, 49, 14, 76, 54, 9, 8, 47, 38, 22, 59, 34, 25, 16, 48, 53, 32, 5, 78, 57, 50, 79, 30, 24, 82,
-     39, 55, 0, 15, 58, 61, 56, 62, 7, 31, 63, 23),
-    (80, 3, 72, 12, 19, 42, 73, 69, 44, 27, 68, 2, 20, 75, 74, 35, 9, 45, 36, 34, 18, 66, 41, 28, 5, 51, 17, 52, 76, 13, 77, 67, 10,
-     26, 64, 46, 40, 50, 21, 4, 25, 29, 65, 60, 0, 49, 47, 1, 6, 33, 14, 58, 38, 78, 37, 53, 16, 79, 54, 22, 8, 39, 48, 32, 30, 82, 55,
-     24, 59, 31, 61, 7, 57, 23, 15, 62, 63, 56),
-    (80, 3, 19, 69, 68, 42, 44, 73, 72, 35, 27, 10, 4, 12, 41, 51, 67, 45, 50, 34, 75, 66, 20, 13, 18, 1, 33, 52, 65, 28, 74, 26, 2,
-     36, 37, 59, 77, 46, 5, 21, 40, 17, 49, 29, 25, 9, 47, 8, 76, 60, 64, 38, 16, 53, 22, 6, 32, 54, 0, 30, 48, 78, 55, 39, 24, 79, 14,
-     7, 82, 57, 61, 56, 58, 23, 62, 63, 31, 15),
-    (80, 3, 19, 68, 44, 12, 42, 66, 20, 72, 69, 27, 41, 18, 45, 34, 73, 50, 26, 52, 9, 4, 40, 28, 46, 2, 21, 67, 51, 75, 64, 5, 33, 74,
-     10, 25, 35, 36, 29, 1, 53, 47, 32, 13, 65, 17, 49, 0, 6, 77, 16, 37, 76, 48, 60, 59, 24, 38, 30, 54, 22, 14, 39, 8, 79, 55, 78,
-     82, 7, 56, 15, 62, 61, 57, 58, 31, 63, 23),
-    (80, 3, 19, 44, 69, 12, 72, 42, 68, 20, 35, 73, 27, 10, 67, 36, 45, 4, 75, 66, 41, 74, 50, 21, 40, 2, 52, 18, 28, 46, 17, 64, 49,
-     33, 34, 5, 77, 37, 26, 65, 76, 29, 47, 1, 13, 79, 51, 9, 54, 78, 25, 60, 8, 53, 48, 32, 6, 38, 14, 0, 55, 24, 30, 58, 82, 39, 16,
-     22, 61, 56, 23, 62, 31, 7, 57, 59, 15, 63),
-    (80, 19, 3, 72, 44, 68, 42, 74, 27, 20, 4, 35, 10, 41, 69, 52, 73, 36, 66, 45, 51, 18, 12, 2, 67, 28, 26, 46, 33, 75, 40, 49, 5,
-     64, 60, 13, 29, 76, 65, 21, 47, 34, 37, 53, 77, 9, 1, 16, 78, 14, 54, 38, 50, 48, 59, 0, 79, 30, 22, 17, 6, 32, 82, 39, 55, 25,
-     61, 24, 58, 57, 8, 23, 15, 63, 7, 62, 56, 31),
-    (3, 19, 68, 69, 73, 72, 12, 42, 44, 10, 18, 45, 41, 27, 67, 66, 4, 26, 36, 20, 2, 9, 50, 28, 46, 34, 64, 13, 74, 37, 52, 53, 49,
-     75, 1, 25, 17, 29, 47, 21, 54, 5, 76, 61, 77, 60, 65, 35, 40, 39, 33, 55, 6, 58, 38, 22, 78, 14, 51, 79, 30, 48, 82, 32, 0, 57,
-     23, 62, 31, 7, 59, 15, 8, 16, 56, 63, 24),
+    (80, 19, 81, 68, 51, 44, 3, 72, 10, 69, 35, 73, 42, 27, 45, 66, 52, 67, 36, 75, 2, 74, 18, 50, 4, 20, 34, 41, 53, 26, 28, 46, 5,
+     64, 12, 76, 17, 37, 40, 1, 21, 65, 78, 77, 47, 25, 33, 29, 9, 13, 54, 23, 48, 32, 38, 24, 6, 49, 79, 7, 8, 60, 39, 55, 0, 15, 82,
+     14, 61, 16, 22, 59, 56, 62, 31, 57, 58, 30, 63),
+    (80, 19, 12, 72, 69, 44, 3, 42, 73, 4, 68, 20, 18, 35, 36, 74, 2, 51, 27, 45, 66, 67, 9, 75, 5, 41, 28, 76, 10, 13, 26, 64, 53, 37,
+     46, 1, 22, 40, 21, 61, 49, 77, 65, 17, 78, 6, 33, 47, 16, 14, 25, 52, 38, 79, 32, 48, 30, 50, 82, 29, 0, 54, 24, 34, 57, 59, 39,
+     8, 55, 31, 15, 56, 60, 63, 7, 62, 58, 23),
+    (80, 3, 19, 35, 68, 12, 69, 44, 42, 4, 72, 27, 51, 2, 41, 73, 20, 52, 50, 74, 34, 17, 18, 45, 66, 67, 26, 21, 33, 75, 36, 49, 5,
+     46, 10, 40, 76, 13, 1, 64, 53, 29, 9, 65, 77, 28, 58, 25, 78, 54, 47, 48, 79, 57, 37, 30, 32, 38, 8, 60, 16, 0, 14, 6, 82, 39, 55,
+     24, 61, 22, 31, 23, 56, 62, 59, 15, 7, 63),
+    (80, 3, 68, 19, 42, 12, 51, 44, 72, 18, 4, 10, 20, 73, 69, 50, 74, 41, 45, 27, 26, 28, 21, 1, 67, 40, 75, 34, 49, 46, 29, 16, 25,
+     66, 2, 35, 32, 52, 13, 58, 53, 76, 47, 5, 17, 33, 77, 65, 37, 9, 22, 48, 38, 64, 14, 30, 0, 24, 79, 36, 54, 6, 8, 55, 39, 78, 82,
+     7, 61, 60, 62, 56, 59, 15, 63, 23, 57, 31),
+    (80, 3, 19, 10, 44, 73, 68, 20, 42, 51, 27, 75, 12, 72, 35, 41, 45, 66, 52, 28, 36, 9, 4, 69, 2, 40, 59, 46, 34, 13, 26, 18, 74,
+     50, 67, 64, 25, 21, 49, 29, 5, 17, 77, 47, 76, 48, 6, 33, 65, 54, 24, 32, 38, 1, 60, 37, 14, 78, 53, 22, 79, 0, 16, 30, 39, 8, 55,
+     82, 7, 56, 61, 15, 57, 58, 31, 62, 23, 63),
+    (80, 19, 3, 44, 68, 12, 69, 73, 42, 27, 72, 52, 51, 9, 10, 45, 20, 41, 34, 67, 75, 28, 4, 74, 40, 18, 26, 2, 50, 66, 46, 36, 35, 5,
+     13, 76, 1, 65, 21, 29, 47, 25, 33, 64, 53, 6, 77, 37, 54, 24, 38, 17, 8, 32, 59, 48, 49, 30, 55, 14, 79, 39, 16, 22, 78, 0, 82,
+     31, 57, 58, 23, 60, 62, 61, 56, 7, 63, 15),
+    (80, 3, 19, 44, 42, 69, 73, 51, 35, 27, 12, 4, 10, 68, 18, 67, 72, 75, 45, 26, 41, 66, 2, 20, 46, 28, 5, 36, 52, 74, 77, 40, 13, 8,
+     29, 64, 47, 76, 34, 37, 65, 50, 21, 9, 1, 33, 53, 22, 38, 60, 49, 17, 55, 79, 30, 39, 59, 6, 24, 54, 32, 0, 25, 58, 14, 48, 78,
+     82, 16, 23, 57, 7, 63, 62, 31, 61, 15, 56),
+    (3, 12, 19, 42, 44, 69, 73, 27, 45, 18, 41, 34, 2, 4, 68, 28, 67, 50, 26, 20, 46, 72, 53, 10, 25, 75, 21, 5, 9, 33, 51, 65, 52, 36,
+     29, 66, 37, 1, 17, 74, 6, 77, 47, 13, 49, 76, 58, 22, 38, 60, 64, 40, 30, 78, 35, 54, 14, 39, 57, 55, 79, 32, 48, 59, 82, 15, 7,
+     23, 16, 63, 8, 24, 0, 61, 62, 56, 31),
 )
 
 
@@ -192,7 +192,7 @@
                 last = abs(dy) == far - 1
                 box.send(("g", far if last else dy - step, cut), functools.partial(gblock, dy, cut, part if last else 0, core),
                          functools.partial(to_y, step))
-        box.send(("s", dy, cut), functools.partial(gblock, dy, cut, 0, core), to_sibling)
+        box.send("s", functools.partial(gblock, dy, cut, 0, core), to_sibling)
 
     def rotate(k):
         g = jnp.concatenate([gp[2 * k], gp[2 * k + 1]], axis=1)
@@ -229,9 +229,7 @@
                     box.send(*copy)
                 waiting[step] = None
             elif item == 82:
-                for dy in range(1 - NY // 2, NY // 2 + 1):
-                    for cut in range(GCUTS):
-                        arrive(("s", dy, cut), gblock(dy, cut, 0, 1 - core))
+                arrive("s", gp.at[pl.ds(0, NY)])
                 gathered = True
             elif item >= 64:
                 dy, cut = (item - 64) // 2 - 3, item % 2
@@ -301,11 +299,11 @@
         give[0, rows] = partial_block(order[0], 1 - core, rows).astype(jnp.bfloat16)
         pushed.send(("p", 0, h), functools.partial(lambda r: give.at[0, r], rows), to_sibling, functools.partial(lambda r: got.at[0, r], rows))
     give_block(1)
-    give_block(2)
     own_block(0)
     for h in starts:
         arrive(("p", 0, h), got.at[0, pl.ds(h * PART, PART)])
         push(0 if h in early[0] else 1, 4, h)
+    give_block(2)
     own_block(1)
     own_block(2)
     for distance in (3, 2, 1):

time: 62.1 us -> 61.9 us (level)
  no operation moved by 1% of the time
where the time goes in v4:
time: 61.9 us; the launch traced here: 61.3 us
  Pallas kernels  58.7 us (95%)
  local copies, waits for them, and re-layouts  1.01 us (2%)
  other arithmetic  0.9 us (1%)
  between operations  0.66 us (1%)
    pallas_call x1, Pallas kernels, per_device(): pl.pallas_call(kernel, out_shape=(pltpu.VMEM(block, jnp.bfloat16), pltpu....  58.7 us

profile of v4, /device:TPU:6, one launch (start us, length us, event | category | flops | bytes accessed | tf_op | source)
XLA Modules:
  0.0 61.3 jit_solution(17759136689003176151)
XLA Ops:
  0.6 0.0 copy-start.1
  0.6 58.7 %shard_map.67 = (bf16[192,384]{1,0:T(8,128)(2,1)S(1)}, f32[192,384]{1,0:T(8,128)S(1)}) custom-call(bf16[192,384]{1,0:T(8,128)(2,1)} %grad.1, bf16[192,384]{1,0:T(8,128)(2,1)} %basis.1, f32[192,384]{1,0:T(8,128)} %moment.1, f32[192,384]{1,0:T(8,128)} %second.1), custom_call_target="tpu_custom_call" | custom-call | flops 1811939328 | bytes 2000000 | tf_op jit(solution)/shard_map/pallas_call | solution.py:341
  59.3 0.0 copy-start
  59.4 0.7 %copy.8 = bf16[192,384]{1,0:T(8,128)(2,1)} copy(bf16[192,384]{1,0:T(8,128)(2,1)S(1)} %get-tuple-element.9) | data formatting | bytes 294912
  60.0 0.0 copy-done.1
  60.0 0.3 copy-done
  60.4 0.9 %fusion = (f32[192,384]{1,0:T(8,128)}, f32[192,384]{1,0:T(8,128)}) fusion(f32[192,384]{1,0:T(8,128)S(1)} %get-tuple-element.6, f32[192,384]{1,0:T(8,128)S(1)} %copy-done.1, f32[192,384]{1,0:T(8,128)S(1)} %copy-done), kind=kLoop, calls=%fused_computation.1 | loop fusion | flops 516096 | bytes 1474560 | tf_op jit(solution)/shard_map/add | solution.py:335
Async XLA Ops:
  0.6 59.4 %copy-start.1 = (f32[192,384]{1,0:T(8,128)S(1)}, f32[192,384]{1,0:T(8,128)}, u32[]{:S(2)}) copy-start(f32[192,384]{1,0:T(8,128)} %second.1) | copy-start | bytes 884740
  59.3 1.0 %copy-start = (f32[192,384]{1,0:T(8,128)S(1)}, f32[192,384]{1,0:T(8,128)}, u32[]{:S(2)}) copy-start(f32[192,384]{1,0:T(8,128)} %moment.1) | copy-start | bytes 884740
